TPU v7x, 32 devices: a whole 2x2x4 slice. The times are simulated.
32 devices in a mesh: wall: 4 (over z), span: 8 (over y, x, core).
Axes of the slice: x: 2, y: 2, z: 4, core: 2. Of those that a mesh axis runs over, the one named last changes fastest.
Arguments:
- solution: float32 [5, 125, 8192], P(None, None, ('wall', 'span')), may hold values from -6 to 6
- level_map: int32 [8192], P(('wall', 'span')), may hold values from 0 to 3, as said below
- send_list: int32 [32, 256], P(('wall', 'span')), may hold values from 0 to 1535, as said below
- face_partner: int32 [6, 8192], P(None, ('wall', 'span')), may hold values from 0 to 1791, as said below
- volume_block: float32 [125, 125], replicated
- lift_block: float32 [125, 150], replicated, may hold values from -0.5 to 0.5
- flux_mixing: float32 [5, 5], replicated
- metric_scale: float32 [8192], P(('wall', 'span')), may hold values from 0.5 to 2
Outputs:
- advanced_solution: float32 [5, 125, 8192], P(None, None, ('wall', 'span'))
Inputs may be any that keep to these rules, and one draw needn't show every extreme that they name: `level_map`: each partition holds elements of every level. `send_list`: slot k (of 8) from any sender to any receiver names a face of a sender's element of level max(3 - j, 0), where j is the largest whole number with 2**j * (8 - k) <= 8. `face_partner`: in each partition's 256 elements, every column of the received traces is named by exactly one face; the other faces name columns of the partition's own trace table.
All inputs are finite; a program needn't handle non-finite values.
Results may differ from a plain program's by a relative error of at most 0.0001.
Values sent between devices are 32-bit elements; how exact they have to be, the bound alone decides.
A program may use at most 64 MiB of HBM per device.

v0:
```python
import jax
import jax.numpy as jnp
from jax import lax
from jax.sharding import PartitionSpec as P

VARIABLES = 5
DEGREE = 4
FACE_NODES = 25
TRACE_ROWS = 125
LEVELS = 4
COARSE_STEPS = 3


COURANT = 0.6


def face_traces(fields):
    local_count = fields.shape[2]
    node_cube = fields.reshape(VARIABLES, DEGREE + 1, DEGREE + 1, DEGREE + 1, local_count)
    face_list = [
        node_cube[:, 0],
        node_cube[:, -1],
        node_cube[:, :, 0],
        node_cube[:, :, -1],
        node_cube[:, :, :, 0],
        node_cube[:, :, :, -1],
    ]
    return jnp.stack(
        [face.reshape(VARIABLES, FACE_NODES, local_count) for face in face_list], axis=1
    )


def tendency(fields, nearby, volume_block, lift_block, flux_mixing, metric_scale):
    own_trace = face_traces(fields).reshape(VARIABLES, 6 * FACE_NODES, fields.shape[2])
    face_jumps = nearby - own_trace
    combined = jnp.einsum("pj,vje->vpe", lift_block, face_jumps, precision=lax.Precision.HIGHEST)
    combined = combined - jnp.einsum(
        "pq,vqe->vpe", volume_block, fields, precision=lax.Precision.HIGHEST
    )
    return metric_scale * jnp.einsum(
        "vw,wpe->vpe", flux_mixing, combined, precision=lax.Precision.HIGHEST
    )


def arrange(columns, local_count):
    shaped = columns.reshape(VARIABLES, FACE_NODES, 6, local_count).transpose(0, 2, 1, 3)
    return shaped.reshape(VARIABLES, 6 * FACE_NODES, local_count)


def make_table(fields):
    return face_traces(fields).transpose(0, 2, 1, 3).reshape(TRACE_ROWS, 6 * fields.shape[2])


def send_slots(outgoing):
    return lax.all_to_all(outgoing, ("wall", "span"), split_axis=1, concat_axis=1, tiled=True)


def lowest_level(substep):
    for candidate in range(LEVELS):
        if substep % 2 ** (LEVELS - 1 - candidate) == 0:
            return candidate
    return LEVELS - 1


def body(
    solution,
    level_map,
    send_list,
    face_partner,
    volume_block,
    lift_block,
    flux_mixing,
    metric_scale,
):
    local_count = solution.shape[2]
    peers = lax.axis_size(("wall", "span"))
    slot_count = send_list.shape[1] // peers
    send_row = send_list[0]
    pointers = face_partner.reshape(-1)
    divisors = jnp.power(2, level_map).astype(jnp.float32)
    substeps = 2 ** (LEVELS - 1)
    start_cache = jnp.zeros((TRACE_ROWS, peers, slot_count), jnp.float32)

    def coarse_step(coarse_index, carry):
        fields, cache = carry
        element_rates = metric_scale * (1.0 + jnp.sqrt(jnp.mean(fields * fields, axis=(0, 1))))
        fastest = lax.pmax(jnp.max(element_rates), ("wall", "span"))
        step_sizes = COURANT / fastest / divisors
        for substep in range(substeps):
            lowest = lowest_level(substep)
            trace_table = make_table(fields)
            outgoing = jnp.take(trace_table, send_row, axis=1).reshape(
                TRACE_ROWS, peers, slot_count
            )
            received = send_slots(outgoing).reshape(TRACE_ROWS, peers * slot_count)
            lookup = jnp.concatenate([trace_table, received], axis=1)
            nearby = arrange(jnp.take(lookup, pointers, axis=1), local_count)
            change = tendency(fields, nearby, volume_block, lift_block, flux_mixing, metric_scale)
            fields = fields + jnp.where(level_map >= lowest, step_sizes * change, 0.0)
        return (fields, cache)

    final_fields, final_cache = lax.fori_loop(0, COARSE_STEPS, coarse_step, (solution, start_cache))
    return final_fields


def solution(mesh):
    return jax.shard_map(
        body,
        mesh=mesh,
        in_specs=(
            P(None, None, ("wall", "span")),
            P(("wall", "span")),
            P(("wall", "span"), None),
            P(None, ("wall", "span")),
            P(),
            P(),
            P(),
            P(("wall", "span")),
        ),
        out_specs=P(None, None, ("wall", "span")),
        check_vma=False,
    )
```

profile of v0, /device:TPU:0, one launch (start us, length us, event | category | flops | bytes accessed | tf_op | source)
XLA Modules:
  0.0 914.7 jit_solution(6604295537766205793)
XLA Ops:
  4.0 908.2 %while.10 = (s32[]{:T(128)}, f32[5,125,256]{2,0,1:T(8,128)}, s32[256]{0:T(256)S(1)}, f32[256]{0:T(256)S(1)}, f32[256]{0:T(256)S(1)}, /*index=5*/s32[256]{0:T(256...) while((s32[]{:T(128)}, f32[5,125,256]{2,0,1:T(8,128)}, ...), condition=%wide.region_4.0_spmd, body=%wide.region_0.6_spmd.sunk | while | flops 4312661504 | bytes 275157792 | solution.py:102
  11.5 7.3 all-to-all-start
  19.4 40.7 %pmax.8 = f32[]{:T(128)} all-reduce(f32[]{:T(128)} %multiply_reduce_fusion.5), channel_id=1, replica_groups=mesh['wall'=4,'span'=8] {'wall','span'}, use_global_device_ids=true, to_apply=%region_3.3 | all-reduce | flops 1 | bytes 8 | tf_op jit(solution)/shard_map/while/body/eval_jaxpr/pmax | solution.py:87
  82.3 5.0 all-to-all-start.1
  89.1 6.5 all-to-all-done.1
  96.7 3.7 gather_fusion.3
  123.0 6.5 all-to-all-done.2
  157.2 6.5 all-to-all-done.3
  183.3 6.5 all-to-all-done.4
  191.0 3.7 gather_fusion.9
  217.1 6.5 all-to-all-done.5
  251.0 6.5 all-to-all-done.6
  285.0 6.5 all-to-all-done.7
  292.7 3.7 gather_fusion.15
  320.5 40.7 %pmax.8 = f32[]{:T(128)} all-reduce(f32[]{:T(128)} %multiply_reduce_fusion.5), channel_id=1, replica_groups=mesh['wall'=4,'span'=8] {'wall','span'}, use_global_device_ids=true, to_apply=%region_3.3 | all-reduce | flops 1 | bytes 8 | tf_op jit(solution)/shard_map/while/body/eval_jaxpr/pmax | solution.py:87
  383.4 4.9 all-to-all-start.1
  390.1 6.5 all-to-all-done.1
  423.9 6.5 all-to-all-done.2
  457.9 6.5 all-to-all-done.3
  484.0 6.5 all-to-all-done.4
  517.8 6.5 all-to-all-done.5
  551.7 6.5 all-to-all-done.6
  585.7 6.5 all-to-all-done.7
  621.3 40.7 %pmax.8 = f32[]{:T(128)} all-reduce(f32[]{:T(128)} %multiply_reduce_fusion.5), channel_id=1, replica_groups=mesh['wall'=4,'span'=8] {'wall','span'}, use_global_device_ids=true, to_apply=%region_3.3 | all-reduce | flops 1 | bytes 8 | tf_op jit(solution)/shard_map/while/body/eval_jaxpr/pmax | solution.py:87
  684.1 4.9 all-to-all-start.1
  690.8 6.5 all-to-all-done.1
  724.6 6.5 all-to-all-done.2
  758.6 6.5 all-to-all-done.3
  784.8 6.5 all-to-all-done.4
  818.6 6.5 all-to-all-done.5
  852.4 6.5 all-to-all-done.6
  886.5 6.5 all-to-all-done.7
  (809 shorter events, 615.7 us)
Async XLA Ops:
  0.0 3.3 copy-start.17
  0.0 3.3 copy-start.8
  4.0 56.8 %copy-start.22 = (f32[256]{0:T(256)}, f32[256]{0:T(256)S(1)}, u32[]{:S(2)}) copy-start(f32[256]{0:T(256)S(1)} %get-tuple-element.416) | copy-start | bytes 3076 | tf_op jit(solution)/shard_map/while
  11.5 52.3 %all-to-all-start = ((f32[125,32,8]{0,2,1:T(8,128)}), f32[125,32,8]{0,2,1:T(8,128)S(1)}, u32[]{:S(2)}, u32[]{:S(2)}) async-start(f32[125,32,8]{0,2,1:T(8,128)} %select_bitcast_fusion.32), calls=%async_computation | async-start | bytes 262144 | tf_op jit(solution)/shard_map/while/body/eval_jaxpr/all_to_all | solution.py:55
  82.3 13.2 %all-to-all-start.1 = ((f32[125,32,8]{0,2,1:T(8,128)}), f32[125,32,8]{0,2,1:T(8,128)S(1)}, u32[]{:S(2)}, u32[]{:S(2)}) async-start(f32[125,32,8]{0,2,1:T(8,128)} %select_bitcast_fusion.34), calls=%async_computation.1 | async-start | bytes 262144 | tf_op jit(solution)/shard_map/while/body/eval_jaxpr/all_to_all | solution.py:55
  118.3 11.2 %all-to-all-start.2 = ((f32[125,32,8]{0,2,1:T(8,128)}), f32[125,32,8]{0,2,1:T(8,128)S(1)}, u32[]{:S(2)}, u32[]{:S(2)}) async-start(f32[125,32,8]{0,2,1:T(8,128)} %select_bitcast_fusion.36), calls=%async_computation.2 | async-start | bytes 262144 | tf_op jit(solution)/shard_map/while/body/eval_jaxpr/all_to_all | solution.py:55
  145.9 9.6 %copy-start = (f32[5,125,256]{2,0,1:T(8,128)}, f32[5,125,256]{2,0,1:T(8,128)S(1)}, u32[]{:S(2)}) copy-start(f32[5,125,256]{2,0,1:T(8,128)S(1)} %fusion.285) | copy-start | bytes 1920004 | tf_op jit(solution)/shard_map/while
  152.2 11.4 %all-to-all-start.3 = ((f32[125,32,8]{0,2,1:T(8,128)}), f32[125,32,8]{0,2,1:T(8,128)S(1)}, u32[]{:S(2)}, u32[]{:S(2)}) async-start(f32[125,32,8]{0,2,1:T(8,128)} %select_bitcast_fusion.38), calls=%async_computation.3 | async-start | bytes 262144 | tf_op jit(solution)/shard_map/while/body/eval_jaxpr/all_to_all | solution.py:55
  178.9 11.0 %all-to-all-start.4 = ((f32[125,32,8]{0,2,1:T(8,128)}), f32[125,32,8]{0,2,1:T(8,128)S(1)}, u32[]{:S(2)}, u32[]{:S(2)}) async-start(f32[125,32,8]{0,2,1:T(8,128)} %select_bitcast_fusion.40), calls=%async_computation.4 | async-start | bytes 262144 | tf_op jit(solution)/shard_map/while/body/eval_jaxpr/all_to_all | solution.py:55
  212.6 11.0 %all-to-all-start.5 = ((f32[125,32,8]{0,2,1:T(8,128)}), f32[125,32,8]{0,2,1:T(8,128)S(1)}, u32[]{:S(2)}, u32[]{:S(2)}) async-start(f32[125,32,8]{0,2,1:T(8,128)} %select_bitcast_fusion.42), calls=%async_computation.5 | async-start | bytes 262144 | tf_op jit(solution)/shard_map/while/body/eval_jaxpr/all_to_all | solution.py:55
  246.4 11.0 %all-to-all-start.6 = ((f32[125,32,8]{0,2,1:T(8,128)}), f32[125,32,8]{0,2,1:T(8,128)S(1)}, u32[]{:S(2)}, u32[]{:S(2)}) async-start(f32[125,32,8]{0,2,1:T(8,128)} %select_bitcast_fusion.44), calls=%async_computation.6 | async-start | bytes 262144 | tf_op jit(solution)/shard_map/while/body/eval_jaxpr/all_to_all | solution.py:55
  280.2 11.3 %all-to-all-start.7 = ((f32[125,32,8]{0,2,1:T(8,128)}), f32[125,32,8]{0,2,1:T(8,128)S(1)}, u32[]{:S(2)}, u32[]{:S(2)}) async-start(f32[125,32,8]{0,2,1:T(8,128)} %select_bitcast_fusion.46), calls=%async_computation.7 | async-start | bytes 262144 | tf_op jit(solution)/shard_map/while/body/eval_jaxpr/all_to_all | solution.py:55
  309.9 52.1 %copy-start.22 = (f32[256]{0:T(256)}, f32[256]{0:T(256)S(1)}, u32[]{:S(2)}) copy-start(f32[256]{0:T(256)S(1)} %get-tuple-element.416) | copy-start | bytes 3076 | tf_op jit(solution)/shard_map/while
  317.3 47.6 %all-to-all-start = ((f32[125,32,8]{0,2,1:T(8,128)}), f32[125,32,8]{0,2,1:T(8,128)S(1)}, u32[]{:S(2)}, u32[]{:S(2)}) async-start(f32[125,32,8]{0,2,1:T(8,128)} %select_bitcast_fusion.32), calls=%async_computation | async-start | bytes 262144 | tf_op jit(solution)/shard_map/while/body/eval_jaxpr/all_to_all | solution.py:55
  383.4 13.1 %all-to-all-start.1 = ((f32[125,32,8]{0,2,1:T(8,128)}), f32[125,32,8]{0,2,1:T(8,128)S(1)}, u32[]{:S(2)}, u32[]{:S(2)}) async-start(f32[125,32,8]{0,2,1:T(8,128)} %select_bitcast_fusion.34), calls=%async_computation.1 | async-start | bytes 262144 | tf_op jit(solution)/shard_map/while/body/eval_jaxpr/all_to_all | solution.py:55
  419.3 11.0 %all-to-all-start.2 = ((f32[125,32,8]{0,2,1:T(8,128)}), f32[125,32,8]{0,2,1:T(8,128)S(1)}, u32[]{:S(2)}, u32[]{:S(2)}) async-start(f32[125,32,8]{0,2,1:T(8,128)} %select_bitcast_fusion.36), calls=%async_computation.2 | async-start | bytes 262144 | tf_op jit(solution)/shard_map/while/body/eval_jaxpr/all_to_all | solution.py:55
  446.8 9.4 %copy-start = (f32[5,125,256]{2,0,1:T(8,128)}, f32[5,125,256]{2,0,1:T(8,128)S(1)}, u32[]{:S(2)}) copy-start(f32[5,125,256]{2,0,1:T(8,128)S(1)} %fusion.285) | copy-start | bytes 1920004 | tf_op jit(solution)/shard_map/while
  453.1 11.3 %all-to-all-start.3 = ((f32[125,32,8]{0,2,1:T(8,128)}), f32[125,32,8]{0,2,1:T(8,128)S(1)}, u32[]{:S(2)}, u32[]{:S(2)}) async-start(f32[125,32,8]{0,2,1:T(8,128)} %select_bitcast_fusion.38), calls=%async_computation.3 | async-start | bytes 262144 | tf_op jit(solution)/shard_map/while/body/eval_jaxpr/all_to_all | solution.py:55
  479.6 11.0 %all-to-all-start.4 = ((f32[125,32,8]{0,2,1:T(8,128)}), f32[125,32,8]{0,2,1:T(8,128)S(1)}, u32[]{:S(2)}, u32[]{:S(2)}) async-start(f32[125,32,8]{0,2,1:T(8,128)} %select_bitcast_fusion.40), calls=%async_computation.4 | async-start | bytes 262144 | tf_op jit(solution)/shard_map/while/body/eval_jaxpr/all_to_all | solution.py:55
  513.3 11.0 %all-to-all-start.5 = ((f32[125,32,8]{0,2,1:T(8,128)}), f32[125,32,8]{0,2,1:T(8,128)S(1)}, u32[]{:S(2)}, u32[]{:S(2)}) async-start(f32[125,32,8]{0,2,1:T(8,128)} %select_bitcast_fusion.42), calls=%async_computation.5 | async-start | bytes 262144 | tf_op jit(solution)/shard_map/while/body/eval_jaxpr/all_to_all | solution.py:55
  547.1 11.0 %all-to-all-start.6 = ((f32[125,32,8]{0,2,1:T(8,128)}), f32[125,32,8]{0,2,1:T(8,128)S(1)}, u32[]{:S(2)}, u32[]{:S(2)}) async-start(f32[125,32,8]{0,2,1:T(8,128)} %select_bitcast_fusion.44), calls=%async_computation.6 | async-start | bytes 262144 | tf_op jit(solution)/shard_map/while/body/eval_jaxpr/all_to_all | solution.py:55
  581.0 11.3 %all-to-all-start.7 = ((f32[125,32,8]{0,2,1:T(8,128)}), f32[125,32,8]{0,2,1:T(8,128)S(1)}, u32[]{:S(2)}, u32[]{:S(2)}) async-start(f32[125,32,8]{0,2,1:T(8,128)} %select_bitcast_fusion.46), calls=%async_computation.7 | async-start | bytes 262144 | tf_op jit(solution)/shard_map/while/body/eval_jaxpr/all_to_all | solution.py:55
  610.6 52.1 %copy-start.22 = (f32[256]{0:T(256)}, f32[256]{0:T(256)S(1)}, u32[]{:S(2)}) copy-start(f32[256]{0:T(256)S(1)} %get-tuple-element.416) | copy-start | bytes 3076 | tf_op jit(solution)/shard_map/while
  618.0 47.6 %all-to-all-start = ((f32[125,32,8]{0,2,1:T(8,128)}), f32[125,32,8]{0,2,1:T(8,128)S(1)}, u32[]{:S(2)}, u32[]{:S(2)}) async-start(f32[125,32,8]{0,2,1:T(8,128)} %select_bitcast_fusion.32), calls=%async_computation | async-start | bytes 262144 | tf_op jit(solution)/shard_map/while/body/eval_jaxpr/all_to_all | solution.py:55
  684.1 13.1 %all-to-all-start.1 = ((f32[125,32,8]{0,2,1:T(8,128)}), f32[125,32,8]{0,2,1:T(8,128)S(1)}, u32[]{:S(2)}, u32[]{:S(2)}) async-start(f32[125,32,8]{0,2,1:T(8,128)} %select_bitcast_fusion.34), calls=%async_computation.1 | async-start | bytes 262144 | tf_op jit(solution)/shard_map/while/body/eval_jaxpr/all_to_all | solution.py:55
  720.0 11.0 %all-to-all-start.2 = ((f32[125,32,8]{0,2,1:T(8,128)}), f32[125,32,8]{0,2,1:T(8,128)S(1)}, u32[]{:S(2)}, u32[]{:S(2)}) async-start(f32[125,32,8]{0,2,1:T(8,128)} %select_bitcast_fusion.36), calls=%async_computation.2 | async-start | bytes 262144 | tf_op jit(solution)/shard_map/while/body/eval_jaxpr/all_to_all | solution.py:55
  747.5 9.4 %copy-start = (f32[5,125,256]{2,0,1:T(8,128)}, f32[5,125,256]{2,0,1:T(8,128)S(1)}, u32[]{:S(2)}) copy-start(f32[5,125,256]{2,0,1:T(8,128)S(1)} %fusion.285) | copy-start | bytes 1920004 | tf_op jit(solution)/shard_map/while
  753.8 11.3 %all-to-all-start.3 = ((f32[125,32,8]{0,2,1:T(8,128)}), f32[125,32,8]{0,2,1:T(8,128)S(1)}, u32[]{:S(2)}, u32[]{:S(2)}) async-start(f32[125,32,8]{0,2,1:T(8,128)} %select_bitcast_fusion.38), calls=%async_computation.3 | async-start | bytes 262144 | tf_op jit(solution)/shard_map/while/body/eval_jaxpr/all_to_all | solution.py:55
  780.3 11.0 %all-to-all-start.4 = ((f32[125,32,8]{0,2,1:T(8,128)}), f32[125,32,8]{0,2,1:T(8,128)S(1)}, u32[]{:S(2)}, u32[]{:S(2)}) async-start(f32[125,32,8]{0,2,1:T(8,128)} %select_bitcast_fusion.40), calls=%async_computation.4 | async-start | bytes 262144 | tf_op jit(solution)/shard_map/while/body/eval_jaxpr/all_to_all | solution.py:55
  814.0 11.0 %all-to-all-start.5 = ((f32[125,32,8]{0,2,1:T(8,128)}), f32[125,32,8]{0,2,1:T(8,128)S(1)}, u32[]{:S(2)}, u32[]{:S(2)}) async-start(f32[125,32,8]{0,2,1:T(8,128)} %select_bitcast_fusion.42), calls=%async_computation.5 | async-start | bytes 262144 | tf_op jit(solution)/shard_map/while/body/eval_jaxpr/all_to_all | solution.py:55
  847.8 11.0 %all-to-all-start.6 = ((f32[125,32,8]{0,2,1:T(8,128)}), f32[125,32,8]{0,2,1:T(8,128)S(1)}, u32[]{:S(2)}, u32[]{:S(2)}) async-start(f32[125,32,8]{0,2,1:T(8,128)} %select_bitcast_fusion.44), calls=%async_computation.6 | async-start | bytes 262144 | tf_op jit(solution)/shard_map/while/body/eval_jaxpr/all_to_all | solution.py:55
  881.7 11.3 %all-to-all-start.7 = ((f32[125,32,8]{0,2,1:T(8,128)}), f32[125,32,8]{0,2,1:T(8,128)S(1)}, u32[]{:S(2)}, u32[]{:S(2)}) async-start(f32[125,32,8]{0,2,1:T(8,128)} %select_bitcast_fusion.46), calls=%async_computation.7 | async-start | bytes 262144 | tf_op jit(solution)/shard_map/while/body/eval_jaxpr/all_to_all | solution.py:55
  (59 other events, 108.4 us)
where the time goes:
time: 923 us; the launch traced here: 915 us
  local copies, waits for them, and re-layouts  309 us (33%)
  matrix products  144 us (16%)
  waiting for transfers between devices  136 us (15%)
  blocking collectives  122 us (13%)
  other arithmetic  116 us (13%)
  starting transfers between devices  79.1 us (9%)
    all_to_all x24, waiting for transfers between devices, send_slots(): lax.all_to_all(outgoing, ('wall', 'span'), split_axis=1, concat_axis=1, t...  136 us
    pmax x3, blocking collectives, coarse_step(): fastest = lax.pmax(jnp.max(element_rates), ('wall', 'span'))  122 us
    gather x24, local copies, waits for them, and re-layouts, coarse_step(): nearby = arrange(jnp.take(lookup, pointers, axis=1), local_count)  85.1 us
    all_to_all x24, starting transfers between devices, send_slots(): lax.all_to_all(outgoing, ('wall', 'span'), split_axis=1, concat_axis=1, t...  79.1 us
    dot_general x24, matrix products, tendency(): jnp.einsum('vw,wpe->vpe', flux_mixing, combined, precision=lax.Precision....  52.2 us
    select_n x27, other arithmetic, coarse_step(): nearby = arrange(jnp.take(lookup, pointers, axis=1), local_count)  46.7 us
    dot_general x24, matrix products, tendency(): jnp.einsum('pj,vje->vpe', lift_block, face_jumps, precision=lax.Precision...  46.5 us
    dot_general x24, matrix products, tendency(): jnp.einsum('pq,vqe->vpe', volume_block, fields, precision=lax.Precision.H...  45.4 us
  transfers between devices with their start and end apart: 24, of which 21 were waited for; matrix products, arithmetic and copies ran while one was open for 5% of the time, Pallas kernels for 0%

commit v1 on v0

v1 whole, which is shorter than its diff:
```python
import functools

import jax
import jax.numpy as jnp
import ml_dtypes
import numpy as np
from jax import lax
from jax.experimental import pallas as pl
from jax.experimental.pallas import tpu as pltpu
from jax.sharding import PartitionSpec as P

VARIABLES = 5
DEGREE = 4
NODES = 125
FACE_NODES = 25
FACES = 6
LEVELS = 4
COARSE_STEPS = 3
SUBSTEPS = 2 ** (LEVELS - 1)
COURANT = 0.6

GROUPS = 4
GROUP = 32
SPARE = GROUP - FACE_NODES
ROWS = GROUPS * GROUP
STACK = FACES * GROUP
RATE_ROW = ROWS - 1
PAD = 128
LAST = VARIABLES - 1

BF16 = jnp.bfloat16
F32 = jnp.float32


def face_nodes():
    cube = np.arange(NODES).reshape(5, 5, 5)
    faces = [cube[0], cube[-1], cube[:, 0], cube[:, -1], cube[:, :, 0], cube[:, :, -1]]
    return np.stack([face.reshape(-1) for face in faces])


def index_blocks():
    nodes = face_nodes()
    pick = np.zeros((GROUPS, STACK, 2 * PAD), np.float32)
    spread = np.zeros((2 * PAD, (GROUPS + 1) * STACK), np.float32)
    own = np.zeros((2 * PAD, PAD), np.float32)
    for face in range(FACES):
        for node in range(FACE_NODES):
            source = face * FACE_NODES + node
            own[source, nodes[face, node]] = 1
            spread[source, face * GROUP + node] = 1
            group, place = divmod(node, SPARE)
            slot = face * GROUP + FACE_NODES + place
            spread[source, (1 + group) * STACK + slot] = 1
            pick[group, slot, PAD + nodes[face, node]] = 1
            for g in range(GROUPS):
                pick[g, face * GROUP + node, nodes[face, node]] = 1
    return tuple(x.astype(ml_dtypes.bfloat16) for x in (pick, spread, own))


def split(x):
    high = x.astype(BF16)
    return high, (x - high.astype(F32)).astype(BF16)


def dot(a, b):
    return jnp.dot(a, b, preferred_element_type=F32)


def kernel(
    peers, span, slots,
    x_ref, level_ref, send_ref, partner_ref, volume_ref, lift_ref, flux_ref, metric_ref,
    pick_ref, spread_ref, own_ref,
    out_ref,
    fields, halves, table, route, send_route, near, near_half, change,
    lift_high, lift_low, vol_high, vol_low, wide, coefs, rate,
    outbox, inbox, send_sem, recv_sem,
):
    local = x_ref.shape[2]
    width = peers * slots
    columns = FACES * local
    me = lax.axis_index("wall") * span + lax.axis_index("span")

    def place_of(peer):
        return (peer // span, lax.rem(peer, span))

    barrier = pltpu.get_barrier_semaphore()

    def greet(i, carry):
        pl.semaphore_signal(
            barrier, inc=1, device_id=place_of(lax.rem(me + i, peers)),
            device_id_type=pl.DeviceIdType.MESH,
        )
        return carry

    lax.fori_loop(1, peers, greet, 0)

    def route_rows(i, carry):
        base = pl.multiple_of(i * 256, 256)
        rows = lax.broadcasted_iota(jnp.int32, (256, local), 0) + base
        for face in range(FACES):
            hit = rows == partner_ref[face : face + 1, :]
            route[pl.ds(base, 256), face * local : (face + 1) * local] = jnp.where(
                hit, 1.0, 0.0
            ).astype(BF16)
        return carry

    lax.fori_loop(0, (columns + width) // 256, route_rows, 0)

    def send_rows(i, carry):
        base = pl.multiple_of(i * 256, 256)
        rows = lax.broadcasted_iota(jnp.int32, (256, width), 0) + base
        send_route[pl.ds(base, 256), :] = jnp.where(rows == send_ref[...], 1.0, 0.0).astype(BF16)
        return carry

    lax.fori_loop(0, columns // 256, send_rows, 0)

    wide[...] = jnp.zeros_like(wide)
    wide[0:NODES, 0 : FACES * FACE_NODES] = lift_ref[...]
    wide_high, wide_low = split(wide[...])
    for half, target in ((wide_high, lift_high), (wide_low, lift_low)):
        spread = dot(half, spread_ref[...]).astype(BF16)
        for g in range(GROUPS):
            target[g, 0:PAD, :] = spread[:, 0:STACK]
            target[g, PAD : 2 * PAD, :] = spread[:, (1 + g) * STACK : (2 + g) * STACK]
    own = dot(wide_high, own_ref[...]) + dot(wide_low, own_ref[...])
    wide[...] = jnp.zeros_like(wide)
    wide[0:NODES, 0:NODES] = volume_ref[...]
    high, low = split(wide[:, 0:PAD] + own)
    vol_high[:, 0:PAD] = high
    vol_high[:, PAD : 2 * PAD] = high
    vol_low[...] = low

    fields[...] = jnp.zeros_like(fields)
    for v in range(VARIABLES):
        fields[v, 0:NODES, :] = x_ref[v]
    rate[...] = jnp.zeros_like(rate)

    pl.semaphore_wait(barrier, peers - 1)

    def substep(step, carry):
        phase = lax.rem(step, SUBSTEPS)
        now = lax.rem(step, 2)

        for v in range(VARIABLES):
            high, low = split(fields[v])
            halves[v, 0:PAD, :] = high
            halves[v, PAD : 2 * PAD, :] = low
        for g in range(GROUPS):
            for half in range(2):
                rows = slice(half * PAD, (half + 1) * PAD)
                both = jnp.concatenate([halves[g, rows, :], halves[LAST, rows, :]], axis=0)
                traces = dot(pick_ref[g], both).astype(BF16)
                for face in range(FACES):
                    table[
                        half * ROWS + g * GROUP : half * ROWS + (g + 1) * GROUP,
                        face * local : (face + 1) * local,
                    ] = traces[face * GROUP : (face + 1) * GROUP, :]

        @pl.when(phase == 0)
        def _():
            total = jnp.zeros((1, local), F32)
            for v in range(VARIABLES):
                total = total + jnp.sum(fields[v] * fields[v], axis=0, keepdims=True)
            rates = metric_ref[...] * (1.0 + jnp.sqrt(total * (1.0 / (VARIABLES * NODES))))
            rate[...] = jnp.broadcast_to(jnp.max(rates, axis=1, keepdims=True), rate.shape)

        chosen = dot(table[...], send_route[...])
        chosen = chosen[0:ROWS, :] + chosen[ROWS : 2 * ROWS, :]
        row_ids = lax.broadcasted_iota(jnp.int32, (ROWS, width), 0)
        chosen = jnp.where(row_ids == RATE_ROW, rate[0:1, 0:1], chosen)
        outbox[now] = chosen.T

        def send(i, carry):
            peer = lax.rem(me + i, peers)
            pltpu.make_async_remote_copy(
                src_ref=outbox.at[now, pl.ds(pl.multiple_of(peer * slots, slots), slots)],
                dst_ref=inbox.at[now, pl.ds(pl.multiple_of(me * slots, slots), slots)],
                send_sem=send_sem.at[now],
                recv_sem=recv_sem.at[now],
                device_id=place_of(peer),
                device_id_type=pl.DeviceIdType.MESH,
            ).start()
            return carry

        lax.fori_loop(1, peers, send, 0)
        mine = pl.ds(pl.multiple_of(me * slots, slots), slots)
        inbox[now, mine, :] = outbox[now, mine, :]

        def near_face(face, carry):
            lanes = pl.ds(pl.multiple_of(face * local, local), local)
            near[:, lanes] = dot(table[...], route[0:columns, lanes])
            return carry

        lax.fori_loop(0, FACES, near_face, 0)
        for v in range(VARIABLES):
            change[v] = dot(vol_high[...], halves[v]) + dot(vol_low[...], halves[v, 0:PAD, :])

        bulk = pl.ds(0, (peers - 1) * slots)
        pltpu.make_async_copy(
            inbox.at[now, bulk], inbox.at[now, bulk], recv_sem.at[now]
        ).wait()
        received = inbox[now].T

        @pl.when(phase == 0)
        def _():
            fastest = jnp.max(received[RATE_ROW : RATE_ROW + 1, :], axis=1, keepdims=True)
            divisors = jnp.left_shift(1, level_ref[...]).astype(F32)
            coefs[...] = COURANT / fastest / divisors

        received = jnp.where(row_ids == RATE_ROW, 0.0, received)
        high, low = split(received)
        received = jnp.concatenate([high, low], axis=0)

        for face in range(FACES):
            lanes = slice(face * local, (face + 1) * local)
            total = near[:, lanes] + dot(received, route[columns : columns + width, lanes])
            near_half[:, lanes] = total.astype(BF16)

        last = jnp.zeros((PAD, local), F32)
        combined = []
        for g in range(GROUPS):
            parts = []
            for half in range(2):
                rows = slice(half * ROWS + g * GROUP, half * ROWS + (g + 1) * GROUP)
                parts.append(
                    jnp.concatenate(
                        [near_half[rows, f * local : (f + 1) * local] for f in range(FACES)],
                        axis=0,
                    )
                )
            lifted = dot(lift_high[g], parts[0])
            lifted = lifted + dot(lift_low[g], parts[0])
            lifted = lifted + dot(lift_high[g], parts[1])
            combined.append(lifted[0:PAD, :] - change[g])
            last = last + lifted[PAD : 2 * PAD, :]
        combined.append(last - change[LAST])
        for v in range(VARIABLES):
            change[v] = combined[v]

        lowest = jnp.where(
            phase == 0, 0, jnp.where(lax.rem(phase, 4) == 0, 1, jnp.where(lax.rem(phase, 2) == 0, 2, 3))
        )
        scale = jnp.where(level_ref[...] >= lowest, coefs[...], 0.0) * metric_ref[...]
        for v in range(VARIABLES):
            mixed = flux_ref[v, 0] * change[0]
            for w in range(1, VARIABLES):
                mixed = mixed + flux_ref[v, w] * change[w]
            fields[v] = fields[v] + scale * mixed

        pltpu.make_async_copy(
            outbox.at[now, bulk], outbox.at[now, bulk], send_sem.at[now]
        ).wait()
        return carry

    lax.fori_loop(0, COARSE_STEPS * SUBSTEPS, substep, 0)
    for v in range(VARIABLES):
        out_ref[v] = fields[v, 0:NODES, :]


def body(x, level_map, send_list, face_partner, volume_block, lift_block, flux_mixing, metric_scale):
    peers = lax.axis_size(("wall", "span"))
    span = lax.axis_size("span")
    local = x.shape[2]
    width = send_list.shape[1]
    slots = width // peers
    columns = FACES * local
    vmem = pl.BlockSpec(memory_space=pltpu.VMEM)
    smem = pl.BlockSpec(memory_space=pltpu.SMEM)
    pick, spread, own = index_blocks()
    return pl.pallas_call(
        functools.partial(kernel, peers, span, slots),
        out_shape=jax.ShapeDtypeStruct(x.shape, x.dtype),
        in_specs=[vmem] * 6 + [smem] + [vmem] * 4,
        out_specs=vmem,
        scratch_shapes=[
            pltpu.VMEM((VARIABLES, PAD, local), F32),
            pltpu.VMEM((VARIABLES, 2 * PAD, local), BF16),
            pltpu.VMEM((2 * ROWS, columns), BF16),
            pltpu.VMEM((columns + width, columns), BF16),
            pltpu.VMEM((columns, width), BF16),
            pltpu.VMEM((2 * ROWS, columns), F32),
            pltpu.VMEM((2 * ROWS, columns), BF16),
            pltpu.VMEM((VARIABLES, PAD, local), F32),
            pltpu.VMEM((GROUPS, 2 * PAD, STACK), BF16),
            pltpu.VMEM((GROUPS, 2 * PAD, STACK), BF16),
            pltpu.VMEM((PAD, 2 * PAD), BF16),
            pltpu.VMEM((PAD, PAD), BF16),
            pltpu.VMEM((PAD, 2 * PAD), F32),
            pltpu.VMEM((1, local), F32),
            pltpu.VMEM((8, 128), F32),
            pltpu.VMEM((2, width, ROWS), F32),
            pltpu.VMEM((2, width, ROWS), F32),
            pltpu.SemaphoreType.DMA((2,)),
            pltpu.SemaphoreType.DMA((2,)),
        ],
        compiler_params=pltpu.CompilerParams(
            collective_id=0, has_side_effects=True, vmem_limit_bytes=48 * 1024 * 1024
        ),
    )(
        x, level_map.reshape(1, local), send_list, face_partner, volume_block, lift_block,
        flux_mixing, metric_scale.reshape(1, local),
        jnp.asarray(pick), jnp.asarray(spread), jnp.asarray(own),
    )


def solution(mesh):
    both = ("wall", "span")
    return jax.shard_map(
        body,
        mesh=mesh,
        in_specs=(
            P(None, None, both), P(both), P(both, None), P(None, both), P(), P(), P(), P(both),
        ),
        out_specs=P(None, None, both),
        check_vma=False,
    )
```

time: 923 us -> 203 us (0.22)
  local copies, waits for them, and re-layouts: 309 us -> 5.09 us
  Pallas kernels: 0 us -> 198 us
  matrix products: 144 us -> 0 us
  waiting for transfers between devices: 136 us -> 0 us
  blocking collectives: 122 us -> 0 us
  other arithmetic: 116 us -> 0 us
  starting transfers between devices: 79.1 us -> 0 us
    pallas_call x0 -> x1, Pallas kernels: none -> 198 us  [body(): pl.pallas_call(functools.partial(kernel, peers, span, slots), out_shape=j...]
    dot_general x72 -> x0, matrix products: 144 us -> none  [the longest x24 52.2 us: tendency(): jnp.einsum('vw,wpe->vpe', flux_mixing, combined, precision=lax.Precision....]
    all_to_all x24 -> x0, waiting for transfers between devices: 136 us -> none  [send_slots(): lax.all_to_all(outgoing, ('wall', 'span'), split_axis=1, concat_axis=1, t...]
    pmax x3 -> x0, blocking collectives: 122 us -> none  [coarse_step(): fastest = lax.pmax(jnp.max(element_rates), ('wall', 'span'))]
    gather x48 -> x0, local copies, waits for them, and re-layouts: 103 us -> none  [the longest x24 85.1 us: coarse_step(): nearby = arrange(jnp.take(lookup, pointers, axis=1), local_count)]
    all_to_all x24 -> x0, starting transfers between devices: 79.1 us -> none  [send_slots(): lax.all_to_all(outgoing, ('wall', 'span'), split_axis=1, concat_axis=1, t...]
    reshape x49 -> x0, local copies, waits for them, and re-layouts: 54 us -> none  [the longest x24 30.2 us: make_table(): face_traces(fields).transpose(0, 2, 1, 3)]
    select_n x30 -> x0, other arithmetic: 46.7 us -> none  [the longest x27 46.7 us: coarse_step(): nearby = arrange(jnp.take(lookup, pointers, axis=1), local_count)]
  transfers between devices with their start and end apart: 24 -> 0, of which waited for: 21 -> 0; matrix products, arithmetic and copies ran while one was open for 5% -> 0% of each run, Pallas kernels for 0% -> 0%
where the time goes in v1:
time: 203 us
  Pallas kernels  198 us (98%)
  local copies, waits for them, and re-layouts  5.09 us (3%)
    pallas_call x1, Pallas kernels, body(): pl.pallas_call(functools.partial(kernel, peers, span, slots), out_shape=j...  198 us
    unnamed x22, local copies, waits for them, and re-layouts  5.09 us

profile of v1, /device:TPU:0, one launch (start us, length us, event | category | flops | bytes accessed | tf_op | source)
XLA Modules:
  0.0 202.8 jit_solution(12259112803806729592)
XLA Ops:
  0.0 0.0 copy-start.3
  0.0 0.0 copy-start.4
  0.0 0.0 copy-start.5
  0.0 0.0 copy-start.6
  0.0 0.0 copy-start.7
  0.0 0.0 copy-start.8
  0.0 0.0 copy-start.9
  0.0 1.1 copy.12.lift_ref
  1.1 0.0 copy-done.3
  1.1 0.0 copy-done.4
  1.2 0.0 copy-done.5
  1.2 0.0 copy-done.6
  1.2 0.0 copy-done.7
  1.2 0.0 copy-done.8
  1.2 0.0 copy-done.9
  1.2 0.0 copy-start
  1.2 1.1 copy-done
  2.3 0.0 copy-start.1
  2.3 1.0 copy-done.1
  3.3 0.0 copy-start.2
  3.3 1.0 copy-done.2
  4.3 197.7 %shard_map.109 = f32[5,125,256]{2,1,0:T(8,128)S(1)} custom-call(f32[5,125,256]{2,1,0:T(8,128)S(1)} %copy-done, s32[1,256]{1,0:T(1,128)S(1)} %bitcast.2, s32[1,256]{1,0:T(1,128)S(1)} %copy-done.8, s32[6,256]{1,0:T(8,128)S(1)} %copy-done.5, f32[125,125]{1,0:T(8,128)S(1)} %copy-done.3, f32[125,150]{1,0:T(8,128)S(1)} %copy.12.lift_ref, f32[5,5]{1,0:T(8,128)S(1)} %copy-done.6, ...), custom_call_target="tpu_custom_call" | custom-call | tf_op jit(solution)/shard_map/pallas_call | solution.py:270
  202.0 0.8 copy.14
Async XLA Ops:
  0.0 1.1 copy-start.3
  0.0 1.1 copy-start.4
  0.0 1.1 copy-start.5
  0.0 1.2 copy-start.6
  0.0 1.2 copy-start.7
  0.0 1.2 copy-start.8
  0.0 1.2 copy-start.9
  1.2 1.1 copy-start
  2.3 1.0 copy-start.1
  3.3 1.0 copy-start.2

commit v2 on v1

--- a/solution.py
+++ b/solution.py
@@ -57,6 +57,16 @@
     return tuple(x.astype(ml_dtypes.bfloat16) for x in (pick, spread, own))
 
 
+def slot_count(slots, lowest):
+    def level(k):
+        power = 0
+        while power < LEVELS - 1 and 2 ** (power + 1) * (slots - k) <= slots:
+            power += 1
+        return LEVELS - 1 - power
+
+    return sum(level(k) >= lowest for k in range(slots))
+
+
 def split(x):
     high = x.astype(BF16)
     return high, (x - high.astype(F32)).astype(BF16)
@@ -73,7 +83,7 @@
     out_ref,
     fields, halves, table, route, send_route, near, near_half, change,
     lift_high, lift_low, vol_high, vol_low, wide, coefs, rate,
-    outbox, inbox, send_sem, recv_sem,
+    outbox, inbox, kept, send_sem, recv_sem,
 ):
     local = x_ref.shape[2]
     width = peers * slots
@@ -134,8 +144,30 @@
     for v in range(VARIABLES):
         fields[v, 0:NODES, :] = x_ref[v]
     rate[...] = jnp.zeros_like(rate)
+    kept[...] = jnp.zeros_like(kept)
 
     pl.semaphore_wait(barrier, peers - 1)
+
+    walls = peers // span
+    my_wall, my_span = lax.axis_index("wall"), lax.axis_index("span")
+    order = []
+    for ahead in sorted(range(walls), key=lambda w: -min(w, walls - w)):
+        wall = my_wall + ahead
+        wall = jnp.where(wall >= walls, wall - walls, wall)
+        for beside in range(span):
+            if ahead or beside:
+                other = my_span + beside
+                order.append((wall, jnp.where(other >= span, other - span, other)))
+
+    fine, middle = slot_count(slots, LEVELS - 1), slot_count(slots, LEVELS - 2)
+
+    def sends(step, phase):
+        first = step == 0
+        odd = lax.rem(phase, 2) == 1
+        part = jnp.logical_and(odd, lax.rem(phase, 4) == 3)
+        whole = jnp.logical_or(first, jnp.logical_and(odd, lax.rem(phase, 4) == 1))
+        few = jnp.logical_and(lax.rem(phase, 2) == 0, step > 0)
+        return ((fine, few), (middle, part), (slots, whole))
 
     def substep(step, carry):
         phase = lax.rem(step, SUBSTEPS)
@@ -170,19 +202,21 @@
         chosen = jnp.where(row_ids == RATE_ROW, rate[0:1, 0:1], chosen)
         outbox[now] = chosen.T
 
-        def send(i, carry):
-            peer = lax.rem(me + i, peers)
-            pltpu.make_async_remote_copy(
-                src_ref=outbox.at[now, pl.ds(pl.multiple_of(peer * slots, slots), slots)],
-                dst_ref=inbox.at[now, pl.ds(pl.multiple_of(me * slots, slots), slots)],
-                send_sem=send_sem.at[now],
-                recv_sem=recv_sem.at[now],
-                device_id=place_of(peer),
-                device_id_type=pl.DeviceIdType.MESH,
-            ).start()
-            return carry
-
-        lax.fori_loop(1, peers, send, 0)
+        for count, chosen_now in sends(step, phase):
+
+            @pl.when(chosen_now)
+            def _(count=count):
+                for there in order:
+                    peer = there[0] * span + there[1]
+                    pltpu.make_async_remote_copy(
+                        src_ref=outbox.at[now, pl.ds(pl.multiple_of(peer * slots, slots), count)],
+                        dst_ref=inbox.at[now, pl.ds(pl.multiple_of(me * slots, slots), count)],
+                        send_sem=send_sem.at[now],
+                        recv_sem=recv_sem.at[now],
+                        device_id=there,
+                        device_id_type=pl.DeviceIdType.MESH,
+                    ).start()
+
         mine = pl.ds(pl.multiple_of(me * slots, slots), slots)
         inbox[now, mine, :] = outbox[now, mine, :]
 
@@ -195,15 +229,25 @@
         for v in range(VARIABLES):
             change[v] = dot(vol_high[...], halves[v]) + dot(vol_low[...], halves[v, 0:PAD, :])
 
-        bulk = pl.ds(0, (peers - 1) * slots)
-        pltpu.make_async_copy(
-            inbox.at[now, bulk], inbox.at[now, bulk], recv_sem.at[now]
-        ).wait()
-        received = inbox[now].T
+        for count, chosen_now in sends(step, phase):
+
+            @pl.when(chosen_now)
+            def _(count=count):
+                bulk = inbox.at[now, pl.ds(0, (peers - 1) * count)]
+                pltpu.make_async_copy(bulk, bulk, recv_sem.at[now]).wait()
+
+        lane_ids = lax.broadcasted_iota(jnp.int32, (ROWS, width), 1)
+        finest = lax.rem(lane_ids, slots) < slot_count(slots, LEVELS - 1)
+        brought = jnp.where(jnp.logical_or(now == 1, step == 0), slots, 0)
+        received = jnp.where(
+            jnp.logical_or(finest, lax.rem(lane_ids, slots) < brought), inbox[now].T, kept[...]
+        )
+        kept[...] = received
 
         @pl.when(phase == 0)
         def _():
-            fastest = jnp.max(received[RATE_ROW : RATE_ROW + 1, :], axis=1, keepdims=True)
+            fresh = jnp.where(finest[0:1, :], received[RATE_ROW : RATE_ROW + 1, :], 0.0)
+            fastest = jnp.max(fresh, axis=1, keepdims=True)
             divisors = jnp.left_shift(1, level_ref[...]).astype(F32)
             coefs[...] = COURANT / fastest / divisors
 
@@ -247,9 +291,13 @@
                 mixed = mixed + flux_ref[v, w] * change[w]
             fields[v] = fields[v] + scale * mixed
 
-        pltpu.make_async_copy(
-            outbox.at[now, bulk], outbox.at[now, bulk], send_sem.at[now]
-        ).wait()
+        for count, chosen_now in sends(step, phase):
+
+            @pl.when(chosen_now)
+            def _(count=count):
+                bulk = outbox.at[now, pl.ds(0, (peers - 1) * count)]
+                pltpu.make_async_copy(bulk, bulk, send_sem.at[now]).wait()
+
         return carry
 
     lax.fori_loop(0, COARSE_STEPS * SUBSTEPS, substep, 0)
@@ -290,6 +338,7 @@
             pltpu.VMEM((8, 128), F32),
             pltpu.VMEM((2, width, ROWS), F32),
             pltpu.VMEM((2, width, ROWS), F32),
+            pltpu.VMEM((ROWS, width), F32),
             pltpu.SemaphoreType.DMA((2,)),
             pltpu.SemaphoreType.DMA((2,)),
         ],

time: 203 us -> 192 us (0.946)
  Pallas kernels: 198 us -> 187 us
    pallas_call x1, Pallas kernels: 198 us -> 187 us  [body(): pl.pallas_call(functools.partial(kernel, peers, span, slots), out_shape=j...]
where the time goes in v2:
time: 192 us
  Pallas kernels  187 us (97%)
  local copies, waits for them, and re-layouts  5.09 us (3%)
    pallas_call x1, Pallas kernels, body(): pl.pallas_call(functools.partial(kernel, peers, span, slots), out_shape=j...  187 us
    unnamed x22, local copies, waits for them, and re-layouts  5.09 us

profile of v2, /device:TPU:0, one launch (start us, length us, event | category | flops | bytes accessed | tf_op | source)
XLA Modules:
  0.0 192.1 jit_solution(5904259628805588317)
XLA Ops:
  0.0 0.0 copy-start.3
  0.0 0.0 copy-start.4
  0.0 0.0 copy-start.5
  0.0 0.0 copy-start.6
  0.0 0.0 copy-start.7
  0.0 0.0 copy-start.8
  0.0 0.0 copy-start.9
  0.0 1.1 copy.12.lift_ref
  1.1 0.0 copy-done.3
  1.1 0.0 copy-done.4
  1.2 0.0 copy-done.5
  1.2 0.0 copy-done.6
  1.2 0.0 copy-done.7
  1.2 0.0 copy-done.8
  1.2 0.0 copy-done.9
  1.2 0.0 copy-start
  1.2 1.1 copy-done
  2.3 0.0 copy-start.1
  2.3 1.0 copy-done.1
  3.3 0.0 copy-start.2
  3.3 1.0 copy-done.2
  4.3 186.9 %shard_map.109 = f32[5,125,256]{2,1,0:T(8,128)S(1)} custom-call(f32[5,125,256]{2,1,0:T(8,128)S(1)} %copy-done, s32[1,256]{1,0:T(1,128)S(1)} %bitcast.2, s32[1,256]{1,0:T(1,128)S(1)} %copy-done.8, s32[6,256]{1,0:T(8,128)S(1)} %copy-done.5, f32[125,125]{1,0:T(8,128)S(1)} %copy-done.3, f32[125,150]{1,0:T(8,128)S(1)} %copy.12.lift_ref, f32[5,5]{1,0:T(8,128)S(1)} %copy-done.6, ...), custom_call_target="tpu_custom_call" | custom-call | tf_op jit(solution)/shard_map/pallas_call | solution.py:318
  191.3 0.8 copy.14
Async XLA Ops:
  0.0 1.1 copy-start.3
  0.0 1.1 copy-start.4
  0.0 1.1 copy-start.5
  0.0 1.2 copy-start.6
  0.0 1.2 copy-start.7
  0.0 1.2 copy-start.8
  0.0 1.2 copy-start.9
  1.2 1.1 copy-start
  2.3 1.0 copy-start.1
  3.3 1.0 copy-start.2

commit v3 on v2

--- a/solution.py
+++ b/solution.py
@@ -25,6 +25,8 @@
 ROWS = GROUPS * GROUP
 STACK = FACES * GROUP
 RATE_ROW = ROWS - 1
+SPREAD = 4
+CHUNK = 16
 PAD = 128
 LAST = VARIABLES - 1
 
@@ -54,7 +56,12 @@
             pick[group, slot, PAD + nodes[face, node]] = 1
             for g in range(GROUPS):
                 pick[g, face * GROUP + node, nodes[face, node]] = 1
-    return tuple(x.astype(ml_dtypes.bfloat16) for x in (pick, spread, own))
+    wide = np.zeros((2 * PAD, SPREAD * 2 * PAD), np.float32)
+    wide[:, : spread.shape[1]] = spread
+    blocks = [pick.reshape(GROUPS * STACK, 2 * PAD)]
+    blocks += [wide[:, i * 2 * PAD : (i + 1) * 2 * PAD] for i in range(SPREAD)]
+    blocks.append(np.pad(own, ((0, 0), (0, PAD))))
+    return np.concatenate(blocks).astype(ml_dtypes.bfloat16)
 
 
 def slot_count(slots, lowest):
@@ -79,11 +86,11 @@
 def kernel(
     peers, span, slots,
     x_ref, level_ref, send_ref, partner_ref, volume_ref, lift_ref, flux_ref, metric_ref,
-    pick_ref, spread_ref, own_ref,
+    index_ref,
     out_ref,
-    fields, halves, table, route, send_route, near, near_half, change,
-    lift_high, lift_low, vol_high, vol_low, wide, coefs, rate,
-    outbox, inbox, kept, send_sem, recv_sem,
+    fields, halves, table, route, send_route, near, near_half, change, lifted,
+    lift_wide, vol_wide, wide, tall, coefs, rate, index,
+    outbox, inbox, kept, send_sem, recv_sem, index_sem,
 ):
     local = x_ref.shape[2]
     width = peers * slots
@@ -93,6 +100,8 @@
     def place_of(peer):
         return (peer // span, lax.rem(peer, span))
 
+    index_copy = pltpu.make_async_copy(index_ref, index, index_sem)
+    index_copy.start()
     barrier = pltpu.get_barrier_semaphore()
 
     def greet(i, carry):
@@ -124,25 +133,38 @@
 
     lax.fori_loop(0, columns // 256, send_rows, 0)
 
-    wide[...] = jnp.zeros_like(wide)
-    wide[0:NODES, 0 : FACES * FACE_NODES] = lift_ref[...]
-    wide_high, wide_low = split(wide[...])
-    for half, target in ((wide_high, lift_high), (wide_low, lift_low)):
-        spread = dot(half, spread_ref[...]).astype(BF16)
+    tall[...] = jnp.zeros_like(tall)
+    tall[0 : FACES * FACE_NODES, 0:NODES] = lift_ref[...]
+    index_copy.wait()
+    wide_halves = split(tall[...].T)
+    first = GROUPS * STACK
+    for place, half in ((0, 0), (1, 1), (2, 0)):
+        spread = jnp.concatenate(
+            [
+                dot(wide_halves[half], index[first + i * 2 * PAD : first + (i + 1) * 2 * PAD, :])
+                for i in range(SPREAD)
+            ],
+            axis=1,
+        ).astype(BF16)
+        lanes = slice(place * STACK, (place + 1) * STACK)
         for g in range(GROUPS):
-            target[g, 0:PAD, :] = spread[:, 0:STACK]
-            target[g, PAD : 2 * PAD, :] = spread[:, (1 + g) * STACK : (2 + g) * STACK]
-    own = dot(wide_high, own_ref[...]) + dot(wide_low, own_ref[...])
+            lift_wide[g, 0:PAD, lanes] = spread[:, 0:STACK]
+            lift_wide[g, PAD : 2 * PAD, lanes] = spread[:, (1 + g) * STACK : (2 + g) * STACK]
+    own_ref = index[first + SPREAD * 2 * PAD :, 0:PAD]
+    own = dot(wide_halves[0], own_ref) + dot(wide_halves[1], own_ref)
     wide[...] = jnp.zeros_like(wide)
     wide[0:NODES, 0:NODES] = volume_ref[...]
-    high, low = split(wide[:, 0:PAD] + own)
-    vol_high[:, 0:PAD] = high
-    vol_high[:, PAD : 2 * PAD] = high
-    vol_low[...] = low
+    high, low = split(wide[...] + own)
+    vol_wide[:, 0:PAD] = high
+    vol_wide[:, PAD : 2 * PAD] = high
+    vol_wide[:, 2 * PAD : 3 * PAD] = low
 
     fields[...] = jnp.zeros_like(fields)
     for v in range(VARIABLES):
         fields[v, 0:NODES, :] = x_ref[v]
+        high, low = split(fields[v])
+        halves[v, 0:PAD, :] = high
+        halves[v, PAD : 2 * PAD, :] = low
     rate[...] = jnp.zeros_like(rate)
     kept[...] = jnp.zeros_like(kept)
 
@@ -173,15 +195,11 @@
         phase = lax.rem(step, SUBSTEPS)
         now = lax.rem(step, 2)
 
-        for v in range(VARIABLES):
-            high, low = split(fields[v])
-            halves[v, 0:PAD, :] = high
-            halves[v, PAD : 2 * PAD, :] = low
         for g in range(GROUPS):
             for half in range(2):
                 rows = slice(half * PAD, (half + 1) * PAD)
                 both = jnp.concatenate([halves[g, rows, :], halves[LAST, rows, :]], axis=0)
-                traces = dot(pick_ref[g], both).astype(BF16)
+                traces = dot(index[g * STACK : (g + 1) * STACK, :], both).astype(BF16)
                 for face in range(FACES):
                     table[
                         half * ROWS + g * GROUP : half * ROWS + (g + 1) * GROUP,
@@ -220,14 +238,13 @@
         mine = pl.ds(pl.multiple_of(me * slots, slots), slots)
         inbox[now, mine, :] = outbox[now, mine, :]
 
-        def near_face(face, carry):
-            lanes = pl.ds(pl.multiple_of(face * local, local), local)
-            near[:, lanes] = dot(table[...], route[0:columns, lanes])
-            return carry
-
-        lax.fori_loop(0, FACES, near_face, 0)
+        for face in range(FACES):
+            lanes = slice(face * local, (face + 1) * local)
+            near[:, lanes] = dot(table[...], route[0:columns, lanes]).astype(BF16)
         for v in range(VARIABLES):
-            change[v] = dot(vol_high[...], halves[v]) + dot(vol_low[...], halves[v, 0:PAD, :])
+            change[v] = dot(
+                vol_wide[...], jnp.concatenate([halves[v], halves[v, 0:PAD, :]], axis=0)
+            )
 
         for count, chosen_now in sends(step, phase):
 
@@ -257,11 +274,9 @@
 
         for face in range(FACES):
             lanes = slice(face * local, (face + 1) * local)
-            total = near[:, lanes] + dot(received, route[columns : columns + width, lanes])
-            near_half[:, lanes] = total.astype(BF16)
-
-        last = jnp.zeros((PAD, local), F32)
-        combined = []
+            far = dot(received, route[columns : columns + width, lanes]).astype(BF16)
+            near_half[:, lanes] = near[:, lanes] + far
+
         for g in range(GROUPS):
             parts = []
             for half in range(2):
@@ -272,24 +287,29 @@
                         axis=0,
                     )
                 )
-            lifted = dot(lift_high[g], parts[0])
-            lifted = lifted + dot(lift_low[g], parts[0])
-            lifted = lifted + dot(lift_high[g], parts[1])
-            combined.append(lifted[0:PAD, :] - change[g])
-            last = last + lifted[PAD : 2 * PAD, :]
-        combined.append(last - change[LAST])
-        for v in range(VARIABLES):
-            change[v] = combined[v]
+            stack = jnp.concatenate([parts[0], parts[0], parts[1]], axis=0)
+            lifted[g] = dot(lift_wide[g], stack)
 
         lowest = jnp.where(
             phase == 0, 0, jnp.where(lax.rem(phase, 4) == 0, 1, jnp.where(lax.rem(phase, 2) == 0, 2, 3))
         )
         scale = jnp.where(level_ref[...] >= lowest, coefs[...], 0.0) * metric_ref[...]
-        for v in range(VARIABLES):
-            mixed = flux_ref[v, 0] * change[0]
-            for w in range(1, VARIABLES):
-                mixed = mixed + flux_ref[v, w] * change[w]
-            fields[v] = fields[v] + scale * mixed
+        for base in range(0, PAD, CHUNK):
+            rows = slice(base, base + CHUNK)
+            combined = [lifted[g, rows, :] - change[g, rows, :] for g in range(GROUPS)]
+            last = lifted[0, PAD + base : PAD + base + CHUNK, :]
+            for g in range(1, GROUPS):
+                last = last + lifted[g, PAD + base : PAD + base + CHUNK, :]
+            combined.append(last - change[LAST, rows, :])
+            for v in range(VARIABLES):
+                mixed = flux_ref[v, 0] * combined[0]
+                for w in range(1, VARIABLES):
+                    mixed = mixed + flux_ref[v, w] * combined[w]
+                moved = fields[v, rows, :] + scale * mixed
+                fields[v, rows, :] = moved
+                high, low = split(moved)
+                halves[v, rows, :] = high
+                halves[v, PAD + base : PAD + base + CHUNK, :] = low
 
         for count, chosen_now in sends(step, phase):
 
@@ -314,11 +334,11 @@
     columns = FACES * local
     vmem = pl.BlockSpec(memory_space=pltpu.VMEM)
     smem = pl.BlockSpec(memory_space=pltpu.SMEM)
-    pick, spread, own = index_blocks()
+    index = index_blocks()
     return pl.pallas_call(
         functools.partial(kernel, peers, span, slots),
         out_shape=jax.ShapeDtypeStruct(x.shape, x.dtype),
-        in_specs=[vmem] * 6 + [smem] + [vmem] * 4,
+        in_specs=[vmem] * 6 + [smem, vmem, pl.BlockSpec(memory_space=pl.ANY)],
         out_specs=vmem,
         scratch_shapes=[
             pltpu.VMEM((VARIABLES, PAD, local), F32),
@@ -326,29 +346,31 @@
             pltpu.VMEM((2 * ROWS, columns), BF16),
             pltpu.VMEM((columns + width, columns), BF16),
             pltpu.VMEM((columns, width), BF16),
-            pltpu.VMEM((2 * ROWS, columns), F32),
+            pltpu.VMEM((2 * ROWS, columns), BF16),
             pltpu.VMEM((2 * ROWS, columns), BF16),
             pltpu.VMEM((VARIABLES, PAD, local), F32),
-            pltpu.VMEM((GROUPS, 2 * PAD, STACK), BF16),
-            pltpu.VMEM((GROUPS, 2 * PAD, STACK), BF16),
-            pltpu.VMEM((PAD, 2 * PAD), BF16),
-            pltpu.VMEM((PAD, PAD), BF16),
-            pltpu.VMEM((PAD, 2 * PAD), F32),
+            pltpu.VMEM((GROUPS, 2 * PAD, local), F32),
+            pltpu.VMEM((GROUPS, 2 * PAD, 3 * STACK), BF16),
+            pltpu.VMEM((PAD, 3 * PAD), BF16),
+            pltpu.VMEM((PAD, PAD), F32),
+            pltpu.VMEM((2 * PAD, PAD), F32),
             pltpu.VMEM((1, local), F32),
             pltpu.VMEM((8, 128), F32),
+            pltpu.VMEM(index.shape, BF16),
             pltpu.VMEM((2, width, ROWS), F32),
             pltpu.VMEM((2, width, ROWS), F32),
             pltpu.VMEM((ROWS, width), F32),
             pltpu.SemaphoreType.DMA((2,)),
             pltpu.SemaphoreType.DMA((2,)),
+            pltpu.SemaphoreType.DMA,
         ],
         compiler_params=pltpu.CompilerParams(
-            collective_id=0, has_side_effects=True, vmem_limit_bytes=48 * 1024 * 1024
+            collective_id=0, has_side_effects=True, vmem_limit_bytes=60 * 1024 * 1024
         ),
     )(
-        x, level_map.reshape(1, local), send_list, face_partner, volume_block, lift_block,
+        x, level_map.reshape(1, local), send_list, face_partner, volume_block, lift_block.T,
         flux_mixing, metric_scale.reshape(1, local),
-        jnp.asarray(pick), jnp.asarray(spread), jnp.asarray(own),
+        jnp.asarray(index),
     )
 
 

time: 192 us -> 194 us (1.010)
  Pallas kernels: 187 us -> 192 us
  local copies, waits for them, and re-layouts: 5.09 us -> 1.99 us
    pallas_call x1, Pallas kernels: 187 us -> 192 us  [body(): pl.pallas_call(functools.partial(kernel, peers, span, slots), out_shape=j...]
    unnamed x22 -> x1, local copies, waits for them, and re-layouts: 5.09 us -> 1.99 us
where the time goes in v3:
time: 194 us
  Pallas kernels  192 us (99%)
  local copies, waits for them, and re-layouts  1.99 us (1%)
    pallas_call x1, Pallas kernels, body(): pl.pallas_call(functools.partial(kernel, peers, span, slots), out_shape=j...  192 us

profile of v3, /device:TPU:0, one launch (start us, length us, event | category | flops | bytes accessed | tf_op | source)
XLA Modules:
  0.0 193.8 jit_solution(17493117816463208494)
XLA Ops:
  0.0 191.8 %shard_map.91 = f32[5,125,256]{2,1,0:T(8,128)} custom-call(f32[5,125,256]{2,1,0:T(8,128)} %x_ref.1, s32[1,256]{1,0:T(1,128)} %bitcast.4, s32[1,256]{1,0:T(1,128)} %send_ref.1, s32[6,256]{1,0:T(8,128)} %partner_ref.1, f32[125,125]{1,0:T(8,128)} %volume_ref.1, f32[150,125]{1,0:T(8,128)} %bitcast.3, f32[5,5]{1,0:T(8,128)} %flux_ref.1, f32[1,256]{1,0:T(1,128)} %bitcast.5, ...), custom_call_target="tpu_custom_call" | custom-call | tf_op jit(solution)/shard_map/pallas_call | solution.py:338
  191.8 2.0 %copy.11 = f32[5,125,256]{2,1,0:T(8,128)} copy(f32[5,125,256]{2,1,0:T(8,128)} %shard_map.91) | data formatting | bytes 1280000

commit v4 on v3

--- a/solution.py
+++ b/solution.py
@@ -88,8 +88,8 @@
     x_ref, level_ref, send_ref, partner_ref, volume_ref, lift_ref, flux_ref, metric_ref,
     index_ref,
     out_ref,
-    fields, halves, table, route, send_route, near, near_half, change, lifted,
-    lift_wide, vol_wide, wide, tall, coefs, rate, index,
+    fields, halves, table, route, send_route, near, far, change, lifted, steady, pairs, pair_near, chosen_lift, chosen, drift, arrived, sent_rows,
+    lift_wide, trace_wide, vol_wide, wide, tall, coefs, rate, step_size, index,
     outbox, inbox, kept, send_sem, recv_sem, index_sem,
 ):
     local = x_ref.shape[2]
@@ -150,6 +150,12 @@
         for g in range(GROUPS):
             lift_wide[g, 0:PAD, lanes] = spread[:, 0:STACK]
             lift_wide[g, PAD : 2 * PAD, lanes] = spread[:, (1 + g) * STACK : (2 + g) * STACK]
+    nodes_of_faces = index[0:STACK, 0:PAD]
+    for g in range(GROUPS):
+        for part in range(2):
+            trace_wide[g, part * STACK : (part + 1) * STACK, :] = dot(
+                nodes_of_faces, lift_wide[g, part * PAD : (part + 1) * PAD, :]
+            ).astype(BF16)
     own_ref = index[first + SPREAD * 2 * PAD :, 0:PAD]
     own = dot(wide_halves[0], own_ref) + dot(wide_halves[1], own_ref)
     wide[...] = jnp.zeros_like(wide)
@@ -167,6 +173,28 @@
         halves[v, PAD : 2 * PAD, :] = low
     rate[...] = jnp.zeros_like(rate)
     kept[...] = jnp.zeros_like(kept)
+
+    element = lax.rem(send_ref[...], local)
+    of_sent = jnp.where(
+        lax.broadcasted_iota(jnp.int32, (local, width), 0) == element, 1.0, 0.0
+    ).astype(BF16)
+    metric = metric_ref[...]
+    top, rest = split(metric)
+    rest_f32 = metric - top.astype(F32)
+    bottom = (rest_f32 - rest.astype(F32)).astype(BF16)
+    pieces = [top, rest, bottom, level_ref[...].astype(F32).astype(BF16)]
+    stacked = jnp.concatenate([jnp.broadcast_to(p.astype(F32), (8, local)) for p in pieces], axis=0)
+    gathered = dot(stacked.astype(BF16), of_sent)
+    sent_rows[0:1, :] = gathered[0:1, :] + gathered[8:9, :] + gathered[16:17, :]
+    sent_rows[1:2, :] = gathered[24:25, :]
+    share = jnp.ones((1, width), F32)
+    for level in range(1, LEVELS):
+        share = jnp.where(gathered[24:25, :] > level - 0.5, 0.5**level, share)
+    sent_rows[2:3, :] = share
+    for face in range(FACES):
+        pairs[:, face * width : (face + 1) * width] = dot(
+            route[columns : columns + width, face * local : (face + 1) * local], of_sent
+        ).astype(BF16)
 
     pl.semaphore_wait(barrier, peers - 1)
 
@@ -191,10 +219,10 @@
         few = jnp.logical_and(lax.rem(phase, 2) == 0, step > 0)
         return ((fine, few), (middle, part), (slots, whole))
 
-    def substep(step, carry):
-        phase = lax.rem(step, SUBSTEPS)
-        now = lax.rem(step, 2)
-
+    row_ids = lax.broadcasted_iota(jnp.int32, (ROWS, width), 0)
+    lane_ids = lax.broadcasted_iota(jnp.int32, (ROWS, width), 1)
+
+    def make_table():
         for g in range(GROUPS):
             for half in range(2):
                 rows = slice(half * PAD, (half + 1) * PAD)
@@ -206,20 +234,55 @@
                         face * local : (face + 1) * local,
                     ] = traces[face * GROUP : (face + 1) * GROUP, :]
 
-        @pl.when(phase == 0)
-        def _():
-            total = jnp.zeros((1, local), F32)
-            for v in range(VARIABLES):
-                total = total + jnp.sum(fields[v] * fields[v], axis=0, keepdims=True)
-            rates = metric_ref[...] * (1.0 + jnp.sqrt(total * (1.0 / (VARIABLES * NODES))))
-            rate[...] = jnp.broadcast_to(jnp.max(rates, axis=1, keepdims=True), rate.shape)
-
-        chosen = dot(table[...], send_route[...])
-        chosen = chosen[0:ROWS, :] + chosen[ROWS : 2 * ROWS, :]
-        row_ids = lax.broadcasted_iota(jnp.int32, (ROWS, width), 0)
-        chosen = jnp.where(row_ids == RATE_ROW, rate[0:1, 0:1], chosen)
-        outbox[now] = chosen.T
-
+    def choose():
+        both = dot(table[...], send_route[...])
+        return both[0:ROWS, :] + both[ROWS : 2 * ROWS, :]
+
+    def stacked_halves(ref, g, count):
+        parts = [
+            jnp.concatenate(
+                [
+                    ref[
+                        half * ROWS + g * GROUP : half * ROWS + (g + 1) * GROUP,
+                        f * count : (f + 1) * count,
+                    ]
+                    for f in range(FACES)
+                ],
+                axis=0,
+            )
+            for half in range(2)
+        ]
+        return jnp.concatenate([parts[0], parts[0], parts[1]], axis=0)
+
+    def mix(values, v):
+        mixed = flux_ref[v, 0] * values[0]
+        for w in range(1, VARIABLES):
+            mixed = mixed + flux_ref[v, w] * values[w]
+        return mixed
+
+    def lifted_rows(base):
+        values = [lifted[g, base : base + CHUNK, :] for g in range(GROUPS)]
+        last = lifted[0, PAD + base : PAD + base + CHUNK, :]
+        for g in range(1, GROUPS):
+            last = last + lifted[g, PAD + base : PAD + base + CHUNK, :]
+        return values + [last]
+
+    def store_halves(v, base, value):
+        high, low = split(value)
+        halves[v, base : base + CHUNK, :] = high
+        halves[v, PAD + base : PAD + base + CHUNK, :] = low
+
+    def set_rate():
+        total = jnp.zeros((1, local), F32)
+        for v in range(VARIABLES):
+            total = total + jnp.sum(fields[v] * fields[v], axis=0, keepdims=True)
+        rates = metric_ref[...] * (1.0 + jnp.sqrt(total * (1.0 / (VARIABLES * NODES))))
+        rate[...] = jnp.broadcast_to(jnp.max(rates, axis=1, keepdims=True), rate.shape)
+
+    def start_sends(step):
+        phase = lax.rem(step, SUBSTEPS)
+        now = lax.rem(step, 2)
+        outbox[now] = jnp.where(row_ids == RATE_ROW, rate[0:1, 0:1], chosen[...]).T
         for count, chosen_now in sends(step, phase):
 
             @pl.when(chosen_now)
@@ -238,6 +301,7 @@
         mine = pl.ds(pl.multiple_of(me * slots, slots), slots)
         inbox[now, mine, :] = outbox[now, mine, :]
 
+    def local_part():
         for face in range(FACES):
             lanes = slice(face * local, (face + 1) * local)
             near[:, lanes] = dot(table[...], route[0:columns, lanes]).astype(BF16)
@@ -245,7 +309,22 @@
             change[v] = dot(
                 vol_wide[...], jnp.concatenate([halves[v], halves[v, 0:PAD, :]], axis=0)
             )
-
+        for g in range(GROUPS):
+            lifted[g] = dot(lift_wide[g], stacked_halves(near, g, local))
+        for base in range(0, PAD, CHUNK):
+            rows = slice(base, base + CHUNK)
+            values = lifted_rows(base)
+            values = [values[v] - change[v, rows, :] for v in range(VARIABLES)]
+            for v in range(VARIABLES):
+                mixed = mix(values, v)
+                steady[v, rows, :] = mixed
+                store_halves(v, base, mixed)
+        make_table()
+        drift[...] = choose()
+
+    def substep(step, carry):
+        phase = lax.rem(step, SUBSTEPS)
+        now = lax.rem(step, 2)
         for count, chosen_now in sends(step, phase):
 
             @pl.when(chosen_now)
@@ -253,7 +332,6 @@
                 bulk = inbox.at[now, pl.ds(0, (peers - 1) * count)]
                 pltpu.make_async_copy(bulk, bulk, recv_sem.at[now]).wait()
 
-        lane_ids = lax.broadcasted_iota(jnp.int32, (ROWS, width), 1)
         finest = lax.rem(lane_ids, slots) < slot_count(slots, LEVELS - 1)
         brought = jnp.where(jnp.logical_or(now == 1, step == 0), slots, 0)
         received = jnp.where(
@@ -264,52 +342,56 @@
         @pl.when(phase == 0)
         def _():
             fresh = jnp.where(finest[0:1, :], received[RATE_ROW : RATE_ROW + 1, :], 0.0)
-            fastest = jnp.max(fresh, axis=1, keepdims=True)
+            step_size[...] = jnp.broadcast_to(
+                COURANT / jnp.max(fresh, axis=1, keepdims=True), step_size.shape
+            )
             divisors = jnp.left_shift(1, level_ref[...]).astype(F32)
-            coefs[...] = COURANT / fastest / divisors
+            coefs[...] = step_size[0:1, 0:1] / divisors
 
         received = jnp.where(row_ids == RATE_ROW, 0.0, received)
         high, low = split(received)
-        received = jnp.concatenate([high, low], axis=0)
-
-        for face in range(FACES):
-            lanes = slice(face * local, (face + 1) * local)
-            far = dot(received, route[columns : columns + width, lanes]).astype(BF16)
-            near_half[:, lanes] = near[:, lanes] + far
-
-        for g in range(GROUPS):
-            parts = []
-            for half in range(2):
-                rows = slice(half * ROWS + g * GROUP, half * ROWS + (g + 1) * GROUP)
-                parts.append(
-                    jnp.concatenate(
-                        [near_half[rows, f * local : (f + 1) * local] for f in range(FACES)],
-                        axis=0,
-                    )
-                )
-            stack = jnp.concatenate([parts[0], parts[0], parts[1]], axis=0)
-            lifted[g] = dot(lift_wide[g], stack)
+        arrived[0:ROWS, :] = high
+        arrived[ROWS : 2 * ROWS, :] = low
 
         lowest = jnp.where(
             phase == 0, 0, jnp.where(lax.rem(phase, 4) == 0, 1, jnp.where(lax.rem(phase, 2) == 0, 2, 3))
         )
-        scale = jnp.where(level_ref[...] >= lowest, coefs[...], 0.0) * metric_ref[...]
-        for base in range(0, PAD, CHUNK):
-            rows = slice(base, base + CHUNK)
-            combined = [lifted[g, rows, :] - change[g, rows, :] for g in range(GROUPS)]
-            last = lifted[0, PAD + base : PAD + base + CHUNK, :]
+
+        for face in range(FACES):
+            lanes = slice(face * width, (face + 1) * width)
+            pair_near[:, lanes] = dot(arrived[...], pairs[:, lanes]).astype(BF16)
+        for g in range(GROUPS):
+            chosen_lift[g] = dot(trace_wide[g], stacked_halves(pair_near, g, width))
+        sent_face = lax.div(send_ref[...], local)
+
+        def at_face(take):
+            total = jnp.zeros((GROUP, width), F32)
+            for face in range(FACES):
+                total = jnp.where(sent_face == face, take(face * GROUP), total)
+            return total
+
+        values = [at_face(lambda row, g=g: chosen_lift[g, row : row + GROUP, :]) for g in range(GROUPS)]
+
+        def last_rows(row):
+            total = chosen_lift[0, STACK + row : STACK + row + GROUP, :]
             for g in range(1, GROUPS):
-                last = last + lifted[g, PAD + base : PAD + base + CHUNK, :]
-            combined.append(last - change[LAST, rows, :])
-            for v in range(VARIABLES):
-                mixed = flux_ref[v, 0] * combined[0]
-                for w in range(1, VARIABLES):
-                    mixed = mixed + flux_ref[v, w] * combined[w]
-                moved = fields[v, rows, :] + scale * mixed
-                fields[v, rows, :] = moved
-                high, low = split(moved)
-                halves[v, rows, :] = high
-                halves[v, PAD + base : PAD + base + CHUNK, :] = low
+                total = total + chosen_lift[g, STACK + row : STACK + row + GROUP, :]
+            return total
+
+        values.append(at_face(last_rows))
+        last = mix(values, LAST)
+        spare = lax.broadcasted_iota(jnp.int32, (GROUP, width), 0) >= FACE_NODES
+        sent_level = sent_rows[1:2, :]
+        sent_scale = jnp.where(
+            sent_level >= lowest.astype(F32),
+            step_size[0:1, 0:1] * sent_rows[2:3, :],
+            0.0,
+        ) * sent_rows[0:1, :]
+        for g in range(GROUPS):
+            rows = slice(g * GROUP, (g + 1) * GROUP)
+            moved = pltpu.roll(last, FACE_NODES - SPARE * g, 0)
+            packed = jnp.where(spare, moved, mix(values, g))
+            chosen[rows, :] = chosen[rows, :] + sent_scale * (drift[rows, :] + packed)
 
         for count, chosen_now in sends(step, phase):
 
@@ -318,9 +400,48 @@
                 bulk = outbox.at[now, pl.ds(0, (peers - 1) * count)]
                 pltpu.make_async_copy(bulk, bulk, send_sem.at[now]).wait()
 
+        more = step + 1 < steps
+        renew = lax.rem(step + 1, SUBSTEPS) == 0
+
+        @pl.when(jnp.logical_and(more, jnp.logical_not(renew)))
+        def _():
+            start_sends(step + 1)
+
+        for face in range(FACES):
+            lanes = slice(face * local, (face + 1) * local)
+            far[:, lanes] = dot(arrived[...], route[columns : columns + width, lanes]).astype(BF16)
+        for g in range(GROUPS):
+            lifted[g] = dot(lift_wide[g], stacked_halves(far, g, local))
+        scale = jnp.where(level_ref[...] >= lowest, coefs[...], 0.0) * metric_ref[...]
+        for base in range(0, PAD, CHUNK):
+            rows = slice(base, base + CHUNK)
+            values = lifted_rows(base)
+            for v in range(VARIABLES):
+                moved = fields[v, rows, :] + scale * (steady[v, rows, :] + mix(values, v))
+                fields[v, rows, :] = moved
+                store_halves(v, base, moved)
+
+        @pl.when(more)
+        def _():
+            make_table()
+
+            @pl.when(renew)
+            def _():
+                set_rate()
+                chosen[...] = choose()
+                start_sends(step + 1)
+
+            local_part()
+
         return carry
 
-    lax.fori_loop(0, COARSE_STEPS * SUBSTEPS, substep, 0)
+    steps = COARSE_STEPS * SUBSTEPS
+    make_table()
+    set_rate()
+    chosen[...] = choose()
+    start_sends(0)
+    local_part()
+    lax.fori_loop(0, steps, substep, 0)
     for v in range(VARIABLES):
         out_ref[v] = fields[v, 0:NODES, :]
 
@@ -350,11 +471,21 @@
             pltpu.VMEM((2 * ROWS, columns), BF16),
             pltpu.VMEM((VARIABLES, PAD, local), F32),
             pltpu.VMEM((GROUPS, 2 * PAD, local), F32),
+            pltpu.VMEM((VARIABLES, PAD, local), F32),
+            pltpu.VMEM((width, FACES * width), BF16),
+            pltpu.VMEM((2 * ROWS, FACES * width), BF16),
+            pltpu.VMEM((GROUPS, 2 * STACK, width), F32),
+            pltpu.VMEM((ROWS, width), F32),
+            pltpu.VMEM((ROWS, width), F32),
+            pltpu.VMEM((2 * ROWS, width), BF16),
+            pltpu.VMEM((8, width), F32),
             pltpu.VMEM((GROUPS, 2 * PAD, 3 * STACK), BF16),
+            pltpu.VMEM((GROUPS, 2 * STACK, 3 * STACK), BF16),
             pltpu.VMEM((PAD, 3 * PAD), BF16),
             pltpu.VMEM((PAD, PAD), F32),
             pltpu.VMEM((2 * PAD, PAD), F32),
             pltpu.VMEM((1, local), F32),
+            pltpu.VMEM((8, 128), F32),
             pltpu.VMEM((8, 128), F32),
             pltpu.VMEM(index.shape, BF16),
             pltpu.VMEM((2, width, ROWS), F32),
@@ -365,7 +496,7 @@
             pltpu.SemaphoreType.DMA,
         ],
         compiler_params=pltpu.CompilerParams(
-            collective_id=0, has_side_effects=True, vmem_limit_bytes=60 * 1024 * 1024
+            collective_id=0, has_side_effects=True, vmem_limit_bytes=56 * 1024 * 1024
         ),
     )(
         x, level_map.reshape(1, local), send_list, face_partner, volume_block, lift_block.T,

time: 194 us -> 191 us (0.985)
  Pallas kernels: 192 us -> 188 us
    pallas_call x1, Pallas kernels: 192 us -> 188 us  [body(): pl.pallas_call(functools.partial(kernel, peers, span, slots), out_shape=j...]
where the time goes in v4:
time: 191 us; the launch traced here: 190 us
  Pallas kernels  188 us (98%)
  local copies, waits for them, and re-layouts  1.99 us (1%)
    pallas_call x1, Pallas kernels, body(): pl.pallas_call(functools.partial(kernel, peers, span, slots), out_shape=j...  188 us

profile of v4, /device:TPU:0, one launch (start us, length us, event | category | flops | bytes accessed | tf_op | source)
XLA Modules:
  0.0 190.5 jit_solution(17327836865586468763)
XLA Ops:
  0.0 188.5 %shard_map.91 = f32[5,125,256]{2,1,0:T(8,128)} custom-call(f32[5,125,256]{2,1,0:T(8,128)} %x_ref.1, s32[1,256]{1,0:T(1,128)} %bitcast.4, s32[1,256]{1,0:T(1,128)} %send_ref.1, s32[6,256]{1,0:T(8,128)} %partner_ref.1, f32[125,125]{1,0:T(8,128)} %volume_ref.1, f32[150,125]{1,0:T(8,128)} %bitcast.3, f32[5,5]{1,0:T(8,128)} %flux_ref.1, f32[1,256]{1,0:T(1,128)} %bitcast.5, ...), custom_call_target="tpu_custom_call" | custom-call | tf_op jit(solution)/shard_map/pallas_call | solution.py:459
  188.5 2.0 %copy.11 = f32[5,125,256]{2,1,0:T(8,128)} copy(f32[5,125,256]{2,1,0:T(8,128)} %shard_map.91) | data formatting | bytes 1280000

commit v5 on v4

--- a/solution.py
+++ b/solution.py
@@ -88,7 +88,7 @@
     x_ref, level_ref, send_ref, partner_ref, volume_ref, lift_ref, flux_ref, metric_ref,
     index_ref,
     out_ref,
-    fields, halves, table, route, send_route, near, far, change, lifted, steady, pairs, pair_near, chosen_lift, chosen, drift, arrived, sent_rows,
+    fields, halves, table, tall_table, route, own_route, send_route, near, far, change, lifted, steady, pairs, pair_near, chosen_lift, chosen, drift, arrived, sent_rows,
     lift_wide, trace_wide, vol_wide, wide, tall, coefs, rate, step_size, index,
     outbox, inbox, kept, send_sem, recv_sem, index_sem,
 ):
@@ -113,17 +113,20 @@
 
     lax.fori_loop(1, peers, greet, 0)
 
-    def route_rows(i, carry):
-        base = pl.multiple_of(i * 256, 256)
-        rows = lax.broadcasted_iota(jnp.int32, (256, local), 0) + base
+    for base in range(0, width, 256):
+        rows = lax.broadcasted_iota(jnp.int32, (256, local), 0) + (columns + base)
         for face in range(FACES):
             hit = rows == partner_ref[face : face + 1, :]
-            route[pl.ds(base, 256), face * local : (face + 1) * local] = jnp.where(
+            route[base : base + 256, face * local : (face + 1) * local] = jnp.where(
                 hit, 1.0, 0.0
             ).astype(BF16)
-        return carry
-
-    lax.fori_loop(0, (columns + width) // 256, route_rows, 0)
+    for face in range(FACES):
+        pointers = jnp.broadcast_to(partner_ref[face : face + 1, :], (128, local)).T[:, 0:1]
+        for base in range(0, columns, 256):
+            lanes = lax.broadcasted_iota(jnp.int32, (local, 256), 1) + base
+            own_route[face * local : (face + 1) * local, base : base + 256] = jnp.where(
+                lanes == pointers, 1.0, 0.0
+            ).astype(BF16)
 
     def send_rows(i, carry):
         base = pl.multiple_of(i * 256, 256)
@@ -193,7 +196,7 @@
     sent_rows[2:3, :] = share
     for face in range(FACES):
         pairs[:, face * width : (face + 1) * width] = dot(
-            route[columns : columns + width, face * local : (face + 1) * local], of_sent
+            route[:, face * local : (face + 1) * local], of_sent
         ).astype(BF16)
 
     pl.semaphore_wait(barrier, peers - 1)
@@ -304,7 +307,11 @@
     def local_part():
         for face in range(FACES):
             lanes = slice(face * local, (face + 1) * local)
-            near[:, lanes] = dot(table[...], route[0:columns, lanes]).astype(BF16)
+            tall_table[lanes, :] = table[:, lanes].T
+        found = dot(own_route[...], tall_table[...])
+        for face in range(FACES):
+            lanes = slice(face * local, (face + 1) * local)
+            near[:, lanes] = found[lanes, :].astype(BF16).T
         for v in range(VARIABLES):
             change[v] = dot(
                 vol_wide[...], jnp.concatenate([halves[v], halves[v, 0:PAD, :]], axis=0)
@@ -409,7 +416,7 @@
 
         for face in range(FACES):
             lanes = slice(face * local, (face + 1) * local)
-            far[:, lanes] = dot(arrived[...], route[columns : columns + width, lanes]).astype(BF16)
+            far[:, lanes] = dot(arrived[...], route[:, lanes]).astype(BF16)
         for g in range(GROUPS):
             lifted[g] = dot(lift_wide[g], stacked_halves(far, g, local))
         scale = jnp.where(level_ref[...] >= lowest, coefs[...], 0.0) * metric_ref[...]
@@ -465,7 +472,9 @@
             pltpu.VMEM((VARIABLES, PAD, local), F32),
             pltpu.VMEM((VARIABLES, 2 * PAD, local), BF16),
             pltpu.VMEM((2 * ROWS, columns), BF16),
-            pltpu.VMEM((columns + width, columns), BF16),
+            pltpu.VMEM((columns, 2 * ROWS), BF16),
+            pltpu.VMEM((width, columns), BF16),
+            pltpu.VMEM((columns, columns), BF16),
             pltpu.VMEM((columns, width), BF16),
             pltpu.VMEM((2 * ROWS, columns), BF16),
             pltpu.VMEM((2 * ROWS, columns), BF16),

time: 191 us -> 216 us (1.13)
  Pallas kernels: 188 us -> 214 us
    pallas_call x1, Pallas kernels: 188 us -> 214 us  [body(): pl.pallas_call(functools.partial(kernel, peers, span, slots), out_shape=j...]
where the time goes in v5:
time: 216 us
  Pallas kernels  214 us (99%)
    pallas_call x1, Pallas kernels, body(): pl.pallas_call(functools.partial(kernel, peers, span, slots), out_shape=j...  214 us

profile of v5, /device:TPU:0, one launch (start us, length us, event | category | flops | bytes accessed | tf_op | source)
XLA Modules:
  0.0 216.2 jit_solution(2223924954537388273)
XLA Ops:
  0.0 214.2 %shard_map.91 = f32[5,125,256]{2,1,0:T(8,128)} custom-call(f32[5,125,256]{2,1,0:T(8,128)} %x_ref.1, s32[1,256]{1,0:T(1,128)} %bitcast.4, s32[1,256]{1,0:T(1,128)} %send_ref.1, s32[6,256]{1,0:T(8,128)} %partner_ref.1, f32[125,125]{1,0:T(8,128)} %volume_ref.1, f32[150,125]{1,0:T(8,128)} %bitcast.3, f32[5,5]{1,0:T(8,128)} %flux_ref.1, f32[1,256]{1,0:T(1,128)} %bitcast.5, ...), custom_call_target="tpu_custom_call" | custom-call | tf_op jit(solution)/shard_map/pallas_call | solution.py:466
  214.2 2.0 copy.11
